TPU v7x, 32 devices: a whole 2x2x4 slice. The times are simulated.
32 devices in a mesh: ctx: 16 (over z, y, x), head: 2 (over core).
Axes of the slice: x: 2, y: 2, z: 4, core: 2. Of those that a mesh axis runs over, the one named last changes fastest.
Arguments:
- query: bfloat16 [6144, 6144], P(('ctx', 'head')), may hold values from -6 to 6
- key_in: bfloat16 [6144, 6144], P(('ctx', 'head')), may hold values from -6 to 6
- value: bfloat16 [6144, 6144], P(('ctx', 'head')), may hold values from -6 to 6
- cotangent: bfloat16 [6144, 6144], P(('ctx', 'head')), may hold values from -18 to 18
- decay_rate: float32 [48, 16], replicated, as said below
- residue: float32 [48, 16], replicated, may hold values from -2 to 2
Outputs:
- mixed: bfloat16 [6144, 6144], P(('ctx', 'head'))
- grad_query: bfloat16 [6144, 6144], P(('ctx', 'head'))
- grad_key: bfloat16 [6144, 6144], P(('ctx', 'head'))
- grad_value: bfloat16 [6144, 6144], P(('ctx', 'head'))
- residue_grad: float32 [48, 16], P('head')
Inputs may be any that keep to these rules, and one draw needn't show every extreme that they name: `decay_rate`: positive decay rates of at most 1/30.
All inputs are finite; a program needn't handle non-finite values.
Results may differ from a plain program's by a relative error of at most 0.00105.
Values may be sent and summed in bfloat16 or wider, within the bound.
A program may use at most 192 MiB of HBM per device.

v0:
```python
import math

import jax
import jax.numpy as jnp
from jax import lax
from jax.sharding import PartitionSpec as P

HEAD_DIM = 128
SPAN = 768


HIGHEST = lax.Precision.HIGHEST


def entering_2(part, axis, combine, identity, reverse):
    count = lax.axis_size(axis)
    place = lax.axis_index(axis)
    ahead = count - 1 - place if reverse else place
    gathered = jax.tree.map(lambda a: lax.all_gather(a, axis), part)
    state = jax.tree.map(lambda a, e: jnp.zeros_like(a) + jnp.asarray(e, a.dtype), part, identity)

    def one(lap, state):
        source = count - 1 - lap if reverse else lap
        return combine(
            state, jax.tree.map(lambda a: lax.dynamic_index_in_dim(a, source, 0, False), gathered)
        )

    return lax.fori_loop(0, ahead, one, state)


def combine_states(earlier, later_part):
    return (earlier[0] * later_part[0], later_part[0][..., None] * earlier[1] + later_part[1])


def modal_layer(
    query,
    key_in,
    value,
    cotangent,
    decay_rate,
    residue,
    block_rows,
    forward_chain,
    backward_chain,
    seq_total,
):
    row_count, feature_count = query.shape
    head_count = decay_rate.shape[0]
    head_size = feature_count // head_count
    block_count = row_count // block_rows

    def blocked(source):
        return source.reshape(block_count, block_rows, head_count, head_size).astype(jnp.float32)

    query_wide = blocked(query)
    key_wide = blocked(key_in)
    value_wide = blocked(value)
    cotan_wide = blocked(cotangent)
    product = key_wide * value_wide
    norm_factor = jnp.sqrt(-jnp.expm1(-2.0 * decay_rate))
    coefficient = residue * norm_factor
    offsets = jnp.arange(block_rows, dtype=jnp.float32)
    decay_in = jnp.exp(-decay_rate[:, :, None] * offsets)
    decay_end = jnp.exp(-decay_rate[:, :, None] * (float(block_rows - 1) - offsets))
    growth = jnp.exp(decay_rate[:, :, None] * offsets)
    one_step = jnp.exp(-decay_rate)
    lag_index = lax.broadcasted_iota(jnp.int32, (block_rows, block_rows), 0) - lax.broadcasted_iota(
        jnp.int32, (block_rows, block_rows), 1
    )
    lower = lag_index[None] >= 0
    weighted_in = coefficient[:, :, None] * decay_in
    full_table = jnp.einsum("hmi,hmj->hij", weighted_in, growth, precision=HIGHEST)
    toeplitz = jnp.where(lower, full_table, 0.0)
    inner_part = jnp.einsum("hij,bjhc->bihc", toeplitz, product, precision=HIGHEST)
    block_ends = jnp.einsum("hmj,bjhc->bhmc", decay_end, product, precision=HIGHEST)
    block_decay = jnp.exp(-decay_rate * block_rows)[:, :, None]

    def walk_forward(state, block_end):
        return (block_decay * state + block_end, state)

    zero_state = jnp.zeros(block_ends.shape[1:], jnp.float32)
    device_total, entering_local = lax.scan(walk_forward, zero_state, block_ends)
    device_decay = jnp.exp(-decay_rate * row_count)
    incoming = forward_chain(device_decay, device_total)
    block_starts = jnp.arange(block_count, dtype=jnp.float32) * block_rows
    block_powers = jnp.exp(-decay_rate[None] * block_starts[:, None, None])[..., None]
    later_starts = (
        float(block_count - 1) - jnp.arange(block_count, dtype=jnp.float32)
    ) * block_rows
    later_powers = jnp.exp(-decay_rate[None] * later_starts[:, None, None])[..., None]
    entering = entering_local + block_powers * incoming[None]
    inflow = coefficient[:, :, None] * one_step[:, :, None] * decay_in
    outer_part = jnp.einsum("hmi,bhmc->bihc", inflow, entering, precision=HIGHEST)
    convolved = inner_part + outer_part
    mixed = (query_wide * convolved).reshape(row_count, feature_count).astype(jnp.bfloat16)
    grad_conv = cotan_wide * query_wide
    grad_query = (cotan_wide * convolved).reshape(row_count, feature_count).astype(jnp.bfloat16)
    back_inner = jnp.einsum("hij,bihc->bjhc", toeplitz, grad_conv, precision=HIGHEST)
    block_heads = jnp.einsum("hmi,bihc->bhmc", decay_in, grad_conv, precision=HIGHEST)

    def walk_backward(state, block_head):
        return (block_decay * state + block_head, state)

    back_total, later_local = lax.scan(walk_backward, zero_state, block_heads, reverse=True)
    outgoing = backward_chain(device_decay, back_total)
    later_states = later_local + later_powers * outgoing[None]
    outflow = coefficient[:, :, None] * one_step[:, :, None] * decay_end
    back_outer = jnp.einsum("hmj,bhmc->bjhc", outflow, later_states, precision=HIGHEST)
    grad_product = back_inner + back_outer
    grad_key = (grad_product * value_wide).reshape(row_count, feature_count).astype(jnp.bfloat16)
    grad_value = (grad_product * key_wide).reshape(row_count, feature_count).astype(jnp.bfloat16)
    cross_table = jnp.einsum("bihc,bjhc->hij", grad_conv, product, precision=HIGHEST)
    cross_lower = jnp.where(lower, cross_table, 0.0)
    grown_rows = jnp.einsum("hij,hmj->hmi", cross_lower, growth, precision=HIGHEST)
    near_terms = jnp.sum(grown_rows * decay_in, axis=2)
    far_terms = one_step * jnp.einsum("bhmc,bhmc->hm", block_heads, entering, precision=HIGHEST)
    residue_terms = norm_factor * (near_terms + far_terms) / math.sqrt(float(seq_total * HEAD_DIM))
    return (mixed, grad_query, grad_key, grad_value, residue_terms)


def on_device(query, key_in, value, cotangent, decay_rate, residue):
    seq_total = query.shape[0] * lax.axis_size("ctx") * lax.axis_size("head")
    group_heads = decay_rate.shape[0] // lax.axis_size("head")
    first_head = lax.axis_index("head") * group_heads
    block_rows = min(SPAN, query.shape[0])

    def forward_chain(decays, totals):
        return entering_2(
            (decays, totals),
            ("ctx", "head"),
            combine_states,
            (jnp.ones_like(decays), jnp.zeros_like(totals)),
            False,
        )[1]

    def backward_chain(decays, totals):
        return entering_2(
            (decays, totals),
            ("ctx", "head"),
            combine_states,
            (jnp.ones_like(decays), jnp.zeros_like(totals)),
            True,
        )[1]

    results = modal_layer(
        query,
        key_in,
        value,
        cotangent,
        decay_rate,
        residue,
        block_rows,
        forward_chain,
        backward_chain,
        seq_total,
    )
    summed = lax.psum(results[4], ("ctx", "head"))
    residue_grad = lax.dynamic_slice_in_dim(summed, first_head, group_heads, 0)
    return (results[0], results[1], results[2], results[3], residue_grad)


def solution(mesh):
    placed = (
        P(("ctx", "head"), None),
        P(("ctx", "head"), None),
        P(("ctx", "head"), None),
        P(("ctx", "head"), None),
        P(),
        P(),
    )
    return jax.shard_map(
        on_device,
        mesh=mesh,
        in_specs=placed,
        out_specs=(
            P(("ctx", "head"), None),
            P(("ctx", "head"), None),
            P(("ctx", "head"), None),
            P(("ctx", "head"), None),
            P("head", None),
        ),
        check_vma=False,
    )
```

profile of v0, /device:TPU:0, one launch (start us, length us, event | category | flops | bytes accessed | tf_op | source)
XLA Modules:
  0.0 370.7 jit_solution(3034369106881262927)
XLA Ops:
  8.6 7.5 %fusion.6 = (f32[24,48,8,128]{3,2,1,0:T(8,128)S(1)}, f32[24,48,8,128]{3,2,1,0:T(8,128)}) fusion(bf16[192,6144]{1,0:T(8,128)(2,1)} %param.12, bf16[192,6144]{1,0:T(8,128)(2,1)} %param.11, bf16[192,6144]{1,0:T(8,128)(2,1)} %param.10, bf16[192,6144]{1,0:T(8,128)(2,1)} %param.13), kind=kLoop, calls=%fused_computation.16 | loop fusion | flops 7077888 | bytes 18874368
  16.1 2.1 copy-done.1
  18.2 5.0 %fusion.45 = f32[1,48,16,128]{3,2,1,0:T(8,128)} fusion(f32[24,48,8,128]{3,2,1,0:T(8,128)S(1)} %get-tuple-element.233, f32[192]{0:T(256)S(1)} %iota_subtract_fusion, f32[48,16]{1,0:T(8,128)S(1)} %get-tuple-element.230, f32[48,16]{1,0:T(8,128)S(1)} %get-tuple-element.229), kind=kOutput, calls=%fused_computation.57 | convolution fusion | flops 226738176 | bytes 5118720 | tf_op jit(solution)/shard_map/hmj,bjhc->bhmc/dot_general | solution.py:75
  23.3 44.7 %all-gather.1 = f32[32,48,16]{1,2,0:T(8,128)S(1)} all-gather(f32[1,48,16]{1,2,0:T(8,128)S(1)} %copy.52), channel_id=2, replica_groups=mesh['ctx'=16,'head'=2] {'ctx','head'}, dimensions={0}, use_global_device_ids=true | all-gather | bytes 101376 | tf_op jit(solution)/shard_map/all_gather | solution.py:19
  68.3 54.2 %all-gather.5.cloned.1.call-done = f32[32,48,16,128]{3,2,1,0:T(8,128)} async-done(((f32[1,48,16,128]{3,2,1,0:T(8,128)}), f32[32,48,16,128]{3,2,1,0:T(8,128)}) %all-gather.5.cloned.1.call-update) | async-done | bytes 12582928 | tf_op jit(solution)/shard_map/all_gather | solution.py:19
  122.8 6.9 %fusion.52 = (f32[48,16]{1,0:T(8,128)}, f32[48,128,16]{1,2,0:T(8,128)S(1)}) fusion(f32[48,16,128]{2,1,0:T(8,128)S(1)} %get-tuple-element.163, f32[48,16]{1,0:T(8,128)} %get-tuple-element.227, f32[48,16]{1,0:T(8,128)} %copy-done.6, f32[24,48,8,128]{3,2,1,0:T(8,128)} %get-tuple-element.234), kind=kOutput, calls=%fused_computation.66 | convolution fusion | flops 226934016 | bytes 5514240 | tf_op jit(solution)/shard_map/hmi,bihc->bhmc/dot_general | solution.py:99
  131.9 3.0 copy.81
  135.5 3.0 copy.83
  139.0 2.9 copy.77
  142.5 2.9 copy.79
  145.5 11.4 %fusion.8 = f32[48,192,192]{2,1,0:T(8,128)S(1)} fusion(f32[24,48,8,128]{3,2,1,0:T(8,128)} %get-tuple-element.234, f32[24,48,8,128]{3,2,1,0:T(8,128)} %copy-done.1), kind=kOutput, calls=%fused_computation.18 | convolution fusion | flops 2717908992 | bytes 16515072 | tf_op jit(solution)/shard_map/bihc,bjhc->hij/dot_general | solution.py:112
  156.9 7.9 %fusion.39 = f32[48,16]{1,0:T(8,128)S(1)} fusion(f32[48,192,192]{2,1,0:T(8,128)S(1)} %fusion.8, pred[192,192]{1,0:T(8,128)(4,1)S(1)} %subtract_compare_fusion, f32[48,16]{1,0:T(8,128)S(1)} %copy-done.9, f32[48,16]{1,0:T(8,128)S(1)} %copy-done.7), kind=kOutput, calls=%fused_computation.55 | convolution fusion | flops 342097152 | bytes 7123968 | tf_op jit(solution)/shard_map/hij,hmj->hmi/dot_general | solution.py:114
  164.9 8.6 %fusion.50 = f32[48,192,192]{2,1,0:T(8,128)S(1)} fusion(f32[48,16]{1,0:T(8,128)S(1)} %copy-done.9, f32[48,16]{1,0:T(8,128)S(1)} %copy-done.7, f32[48,16]{1,0:T(8,128)S(1)} %get-tuple-element.221), kind=kOutput, calls=%fused_computation.62 | convolution fusion | flops 340180992 | bytes 7087104 | tf_op jit(solution)/shard_map/hmi,hmj->hij/dot_general | solution.py:72
  173.6 10.7 %fusion.4 = f32[48,128,192]{1,2,0:T(8,128)} fusion(f32[48,192,192]{2,1,0:T(8,128)S(1)} %fusion.50, pred[192,192]{1,0:T(8,128)(4,1)S(1)} %subtract_compare_fusion, f32[24,48,8,128]{3,2,1,0:T(8,128)S(1)} %bitcast.116), kind=kOutput, calls=%fused_computation.8 | convolution fusion | flops 2719678464 | bytes 16551936 | tf_op jit(solution)/shard_map/hij,bjhc->bihc/dot_general | solution.py:74
  184.3 14.8 %fusion.20 = (bf16[1,192,48,128]{3,1,2,0:T(8,128)(2,1)S(1)}, bf16[1,192,48,128]{3,1,2,0:T(8,128)(2,1)S(1)}) fusion(f32[1,192,48,128]{3,2,1,0:T(8,128)S(1)} %bitcast.124, f32[1,192,48,128]{3,2,1,0:T(8,128)S(1)} %bitcast.121, f32[48,128,192]{1,2,0:T(8,128)} %fusion.4, f32[48,16]{1,0:T(8,128)S(1)} %get-tuple-element.220, f32[48,16]{1,0:T(8,128)S(1)} %copy-done.7, ...), kind=kOutput, calls=%fused_computation.34 | convolution fusion | flops 232783872 | bytes 19276800 | tf_op jit(solution)/shard_map/hmi,bhmc->bihc/dot_general | solution.py:93
  199.2 1.5 copy.58
  200.7 2.0 copy.127
  204.2 2.0 copy.128
  206.2 74.1 %psum.7 = f32[48,16]{1,0:T(8,128)S(1)} all-reduce(f32[48,16]{1,0:T(8,128)S(1)} %get-tuple-element.226), channel_id=1, replica_groups=mesh['ctx'=16,'head'=2] {'ctx','head'}, use_global_device_ids=true, to_apply=%region_5.6 | all-reduce | flops 768 | bytes 6144 | tf_op jit(solution)/shard_map/psum | solution.py:157
  281.0 22.2 %fusion.2 = f32[48,128,192]{1,2,0:T(8,128)} fusion(f32[48,192,192]{2,1,0:T(8,128)} %copy-done, pred[192,192]{1,0:T(8,128)(4,1)S(1)} %subtract_compare_fusion, f32[24,48,8,128]{3,2,1,0:T(8,128)} %get-tuple-element.234), kind=kOutput, calls=%fused_computation.6 | convolution fusion | flops 2719678464 | bytes 16551936 | tf_op jit(solution)/shard_map/hij,bihc->bjhc/dot_general | solution.py:98
  303.3 38.1 %while.17 = (s32[]{:T(128)}, f32[48,16,128]{2,1,0:T(8,128)S(1)}, s32[]{:T(128)}, f32[32,48,16]{2,1,0:T(8,128)S(1)}, f32[32,48,16,128]{3,2,1,0:T(8,128)}, /*index=5*/s32[]{:T(128)}, s32[]{:T(128)}, s32[]{:T(128)}, s32[]{:T(128)}) while((s32[]{:T(128)}, f32[48,16,128]{2,1,0:T(8,128)S(1)}, s32[]{:T(128)}, f32[32,48,16]{2,1,0:T(8,128)S(1)}, ...), condition=%wide.region_3.4_spmd, body=%wide.region_2.3_spmd.sunk | while | flops 196614 | bytes 1189011 | solution.py:28
  341.4 14.9 %fusion.18 = (bf16[1,192,48,128]{3,1,2,0:T(8,128)(2,1)S(1)}, bf16[1,192,48,128]{3,1,2,0:T(8,128)(2,1)S(1)}) fusion(f32[1,192,48,128]{3,2,1,0:T(8,128)} %bitcast.118, f32[1,192,48,128]{3,2,1,0:T(8,128)} %bitcast.117, f32[48,128,192]{1,2,0:T(8,128)} %fusion.2, f32[48,16]{1,0:T(8,128)S(1)} %get-tuple-element.220, f32[192]{0:T(256)S(1)} %iota_subtract_fusion, ...), kind=kOutput, calls=%fused_computation.30 | convolution fusion | flops 232783872 | bytes 19277568 | tf_op jit(solution)/shard_map/hmj,bhmc->bjhc/dot_general | solution.py:108
  357.9 2.0 copy.125
  361.4 2.0 copy.126
  (134 shorter events, 48.1 us)
Async XLA Ops:
  7.2 115.4 %all-gather.5.cloned.1.call-start = ((), (), s32[]{:S(2)}) async-start(), calls=%async_computation | async-start | bytes 12976128 | tf_op jit(solution)/shard_map/all_gather | solution.py:19
  8.0 8.1 %copy-start.8 = (f32[48,16]{1,0:T(8,128)}, f32[48,16]{1,0:T(8,128)S(1)}, u32[]{:S(2)}) copy-start(f32[48,16]{1,0:T(8,128)S(1)} %copy.47) | copy-start | bytes 9220
  8.6 7.5 %copy-start.6 = (f32[48,16]{1,0:T(8,128)}, f32[48,16]{1,0:T(8,128)S(1)}, u32[]{:S(2)}) copy-start(f32[48,16]{1,0:T(8,128)S(1)} %get-tuple-element.230) | copy-start | bytes 9220
  8.6 7.5 %copy-start.11 = (f32[48,16]{1,0:T(8,128)}, f32[48,16]{1,0:T(8,128)S(1)}, u32[]{:S(2)}) copy-start(f32[48,16]{1,0:T(8,128)S(1)} %get-tuple-element.229) | copy-start | bytes 9220
  16.1 2.1 copy-start.1
  23.2 280.1 %all-gather.7.cloned.1.call-start = ((), (), s32[]{:S(2)}) async-start(), calls=%async_computation.1 | async-start | bytes 12976128 | tf_op jit(solution)/shard_map/all_gather | solution.py:19
  122.8 7.0 %copy-start.12 = (f32[48,16]{1,0:T(8,128)S(1)}, f32[48,16]{1,0:T(8,128)}, u32[]{:S(2)}) copy-start(f32[48,16]{1,0:T(8,128)} %copy-done.11) | copy-start | bytes 9220
  122.8 7.9 %copy-start.15 = (f32[48,16]{0,1:T(8,128)S(1)}, f32[48,16]{0,1:T(8,128)}, u32[]{:S(2)}) copy-start(f32[48,16]{0,1:T(8,128)} %param.15) | copy-start | bytes 9220
  122.8 8.6 %copy-start.2 = (bf16[192,6144]{1,0:T(8,128)(2,1)S(1)}, bf16[192,6144]{1,0:T(8,128)(2,1)}, u32[]{:S(2)}) copy-start(bf16[192,6144]{1,0:T(8,128)(2,1)} %param.12) | copy-start | bytes 7077892
  131.9 3.0 copy-start.3
  135.5 3.0 copy-start.4
  139.0 2.9 copy-start.5
  145.4 11.4 %copy-start.7 = (f32[48,16]{1,0:T(8,128)S(1)}, f32[48,16]{1,0:T(8,128)}, u32[]{:S(2)}) copy-start(f32[48,16]{1,0:T(8,128)} %copy-done.6) | copy-start | bytes 9220
  145.5 11.4 %copy-start.9 = (f32[48,16]{1,0:T(8,128)S(1)}, f32[48,16]{1,0:T(8,128)}, u32[]{:S(2)}) copy-start(f32[48,16]{1,0:T(8,128)} %copy-done.8) | copy-start | bytes 9220
  156.9 7.9 %copy-start.13 = (f32[48,16]{1,0:T(8,128)S(1)}, f32[48,16]{1,0:T(8,128)}, u32[]{:S(2)}) copy-start(f32[48,16]{1,0:T(8,128)} %get-tuple-element.231) | copy-start | bytes 9220
  156.9 7.9 %copy-start.14 = (f32[48,16]{1,0:T(8,128)S(1)}, f32[48,16]{1,0:T(8,128)}, u32[]{:S(2)}) copy-start(f32[48,16]{1,0:T(8,128)} %copy.48) | copy-start | bytes 9220
  156.9 16.6 %slice-start = ((s8[4718592]{0:T(1024)(128)(4,1)}), s8[4194304]{0:T(1024)(128)(4,1)S(1)}, s32[]{:S(2)}) async-start(s8[4718592]{0:T(1024)(128)(4,1)} %bitcast.115), calls=%async_computation.2 | async-start | bytes 8388608
  164.8 8.7 %slice-start.1 = ((s8[4718592]{0:T(1024)(128)(4,1)}), s8[524288]{0:T(1024)(128)(4,1)S(1)}, s32[]{:S(2)}) async-start(s8[4718592]{0:T(1024)(128)(4,1)} %bitcast.115), calls=%async_computation.3 | async-start | bytes 1048576
  164.9 19.4 %slice-start.2 = ((s8[4718592]{0:T(1024)(128)(4,1)}), s8[4194304]{0:T(1024)(128)(4,1)S(1)}, s32[]{:S(2)}) async-start(s8[4718592]{0:T(1024)(128)(4,1)} %bitcast.119), calls=%async_computation.4 | async-start | bytes 8388608
  164.9 19.4 %slice-start.4 = ((s8[4718592]{0:T(1024)(128)(4,1)}), s8[4194304]{0:T(1024)(128)(4,1)S(1)}, s32[]{:S(2)}) async-start(s8[4718592]{0:T(1024)(128)(4,1)} %bitcast.122), calls=%async_computation.6 | async-start | bytes 8388608
  173.6 10.7 %copy-start = (f32[48,192,192]{2,1,0:T(8,128)}, f32[48,192,192]{2,1,0:T(8,128)S(1)}, u32[]{:S(2)}) copy-start(f32[48,192,192]{2,1,0:T(8,128)S(1)} %fusion.50) | copy-start | bytes 21233668
  173.6 10.7 %slice-start.3 = ((s8[4718592]{0:T(1024)(128)(4,1)}), s8[524288]{0:T(1024)(128)(4,1)S(1)}, s32[]{:S(2)}) async-start(s8[4718592]{0:T(1024)(128)(4,1)} %bitcast.119), calls=%async_computation.5 | async-start | bytes 1048576
  173.6 10.7 %slice-start.5 = ((s8[4718592]{0:T(1024)(128)(4,1)}), s8[524288]{0:T(1024)(128)(4,1)S(1)}, s32[]{:S(2)}) async-start(s8[4718592]{0:T(1024)(128)(4,1)} %bitcast.122), calls=%async_computation.7 | async-start | bytes 1048576
  173.6 10.7 %copy-start.10 = (f32[48,16]{1,0:T(8,128)S(1)}, f32[48,16]{1,0:T(8,128)}, u32[]{:S(2)}) copy-start(f32[48,16]{1,0:T(8,128)} %get-tuple-element.227) | copy-start | bytes 9220
Sparse Core Ops, SparseCore 0:
  23.3 99.1 all-gather.4
  130.8 132.5 all-gather.6
where the time goes:
time: 377 us; the launch traced here: 371 us
  blocking collectives  119 us (32%)
  matrix products  102 us (27%)
  waiting for transfers between devices  54.2 us (14%)
  other arithmetic  47.8 us (13%)
  local copies, waits for them, and re-layouts  31 us (8%)
  between operations  14.9 us (4%)
    psum x1, blocking collectives, on_device(): summed = lax.psum(results[4], ('ctx', 'head'))  74.1 us
    all_gather x2, waiting for transfers between devices, entering_2(): gathered = jax.tree.map(lambda a: lax.all_gather(a, axis), part)  54.2 us
    all_gather x1, blocking collectives, entering_2(): gathered = jax.tree.map(lambda a: lax.all_gather(a, axis), part)  44.7 us
    add x31, other arithmetic, combine_states(): later_part[0][..., None] * earlier[1] + later_part[1]  36.6 us
    unnamed x56, local copies, waits for them, and re-layouts  24.3 us
    dot_general x1, matrix products, modal_layer(): jnp.einsum('hij,bihc->bjhc', toeplitz, grad_conv, precision=HIGHEST)  22.2 us
    dot_general x1, matrix products, modal_layer(): jnp.einsum('hmj,bhmc->bjhc', outflow, later_states, precision=HIGHEST)  14.9 us
    dot_general x1, matrix products, modal_layer(): jnp.einsum('hmi,bhmc->bihc', inflow, entering, precision=HIGHEST)  14.8 us
  transfers between devices with their start and end apart: 2, of which 1 were waited for; matrix products, arithmetic and copies ran while one was open for 27% of the time, Pallas kernels for 0%

commit v1 on v0

v1 whole, which is shorter than its diff:
```python
import functools
import math

import jax
import jax.numpy as jnp
from jax import lax
from jax.experimental import pallas as pl
from jax.experimental.pallas import tpu as pltpu
from jax.sharding import PartitionSpec as P

F32 = jnp.float32
BF16 = jnp.bfloat16
LAST = (((1,), (1,)), ((), ()))


def split(x):
    high = x.astype(BF16)
    return high, (x - high.astype(F32)).astype(BF16)


def mm(a, b):
    return jnp.dot(a, b, preferred_element_type=F32)


def mm_t(a, b):
    return lax.dot_general(a, b, LAST, preferred_element_type=F32)


def lanes(a, b):
    return jnp.concatenate([a, b], axis=1)


def state_kernel(group, width, poles, q_ref, k_ref, v_ref, c_ref, pc_ref, pr_ref, s_ref, near_ref):
    rows = q_ref.shape[0]
    place_l = lax.broadcasted_iota(jnp.int32, (poles, rows), 1).astype(F32)
    place_s = lax.broadcasted_iota(jnp.int32, (rows, poles), 0).astype(F32)
    lower = lax.broadcasted_iota(jnp.int32, (rows, rows), 0) >= lax.broadcasted_iota(
        jnp.int32, (rows, rows), 1
    )
    for h in range(group):
        cols = slice(h * width, (h + 1) * width)
        rate = pc_ref[h, :, 0:1]
        rate_row = pr_ref[h, 0:1, :poles]
        ph, pl_ = split(k_ref[:, cols].astype(F32) * v_ref[:, cols].astype(F32))
        gh, gl = split(c_ref[:, cols].astype(F32) * q_ref[:, cols].astype(F32))
        for d, (hi, lo, lag) in enumerate(
            ((ph, pl_, rows - 1.0 - place_l), (gh, gl, place_l))
        ):
            wide = mm(jnp.concatenate(split(jnp.exp(-rate * lag)), axis=0), lanes(hi, lo))
            s_ref[0, d, h] = (wide[:poles, :width] + wide[:poles, width:]) + (
                wide[poles:, :width] + wide[poles:, width:]
            )
        cross = mm_t(lanes(gh, gl), lanes(ph, ph)) + mm_t(gh, pl_)
        xh, xl = split(jnp.where(lower, cross, 0.0))
        wh, wl = split(jnp.exp(rate * place_l))
        grown = mm_t(xh, jnp.concatenate([wh, wl], axis=0))
        grown = grown[:, :poles] + grown[:, poles:] + mm_t(xl, wh)
        near_ref[h] = jnp.sum(grown * jnp.exp(-rate_row * place_s), axis=0, keepdims=True)


def chain_kernel(
    near_group, s_ref, near_ref, lam_ref, scale_ref, ent_ref, res_ref,
    pair, npair, chip, plane, tot, zed, back, got, stage, farb, resb,
    pair_s, pair_r, plane_s, plane_r, zed_s, zed_r, back_s, back_r, ent_s, ent_r, res_s, res_r,
):
    core = lax.axis_index("head")
    ctx = lax.axis_index("ctx")
    n_ctx = lax.axis_size("ctx")
    other = 1 - core
    q_n = near_group
    z_n = n_ctx // q_n
    z = ctx // q_n
    q = ctx % q_n

    def remote(src, dst, ss, rs, where):
        return pltpu.make_async_remote_copy(
            src_ref=src, dst_ref=dst, send_sem=ss, recv_sem=rs,
            device_id=where, device_id_type=pl.DeviceIdType.MESH,
        )

    barrier = pltpu.get_barrier_semaphore()
    pl.semaphore_signal(
        barrier, inc=1, device_id=(ctx, other), device_id_type=pl.DeviceIdType.MESH
    )
    for k in range(1, n_ctx):
        pl.semaphore_signal(
            barrier, inc=1, device_id=((ctx + k) % n_ctx, core),
            device_id_type=pl.DeviceIdType.MESH,
        )
    pl.semaphore_wait(barrier, n_ctx)

    first = [
        remote(s_ref.at[other], pair.at[core], pair_s.at[0], pair_r.at[0], (ctx, other)),
        remote(near_ref.at[other], npair.at[core], pair_s.at[1], pair_r.at[1], (ctx, other)),
    ]
    for copy in first:
        copy.start()
    pair[core] = s_ref[core]
    npair[core] = near_ref[core]
    for copy in first:
        copy.wait()

    plane_copies = []
    for k in range(1, q_n + 1):
        to = (q + k) % q_n
        lam = lam_ref[0, core, to]
        chip[to, 0] = lam * pair[0, 0, to] + pair[1, 0, to]
        chip[to, 1] = pair[0, 1, to] + lam * pair[1, 1, to]
        if k < q_n:
            copy = remote(
                chip.at[to], plane.at[q], plane_s.at[to], plane_r.at[q], (z * q_n + to, core)
            )
            copy.start()
            plane_copies.append(copy)
    plane[q] = chip[q]
    for k in range(1, q_n):
        src = (q + k) % q_n
        remote(
            chip.at[src], plane.at[src], plane_s.at[src], plane_r.at[src], (z * q_n + src, core)
        ).wait_recv()
    lam2 = lam_ref[1, core, q]
    fwd = plane[0, 0]
    bwd = plane[q_n - 1, 1]
    for j in range(1, q_n):
        fwd = lam2 * fwd + plane[j, 0]
        bwd = lam2 * bwd + plane[q_n - 1 - j, 1]
    tot[0] = fwd
    tot[1] = bwd
    zed_copies = []
    for k in range(1, z_n):
        to = (z + k) % z_n
        way = (to < z).astype(jnp.int32)
        copy = remote(
            tot.at[way], zed.at[z], zed_s.at[to], zed_r.at[z], (to * q_n + q, core)
        )
        copy.start()
        zed_copies.append(copy)
    zed[z] = jnp.zeros_like(fwd)
    for k in range(1, z_n):
        src = (z + k) % z_n
        remote(
            tot.at[0], zed.at[src], zed_s.at[src], zed_r.at[src], (src * q_n + q, core)
        ).wait_recv()
    lam3 = lam_ref[2, core, q]
    fwd = jnp.zeros_like(fwd)
    bwd = jnp.zeros_like(bwd)
    for j in range(z_n):
        use = (j < z).astype(F32)
        fwd = fwd + use * ((lam3 - 1.0) * fwd + zed[j])
        late = z_n - 1 - j
        use = (late > z).astype(F32)
        bwd = bwd + use * ((lam3 - 1.0) * bwd + zed[late])
    for j in range(q_n):
        back[j, 0] = fwd
        back[q_n - 1 - j, 1] = bwd
        fwd = lam2 * fwd + plane[j, 0]
        bwd = lam2 * bwd + plane[q_n - 1 - j, 1]
    back_copies = []
    for k in range(1, q_n):
        to = (q + k) % q_n
        copy = remote(back.at[to], got.at[q], back_s.at[to], back_r.at[q], (z * q_n + to, core))
        copy.start()
        back_copies.append(copy)
    got[q] = back[q]
    for k in range(1, q_n):
        src = (q + k) % q_n
        remote(
            back.at[src], got.at[src], back_s.at[src], back_r.at[src], (z * q_n + src, core)
        ).wait_recv()

    for j in range(q_n):
        lam = lam_ref[0, core, j]
        fwd = got[j, 0]
        bwd = got[j, 1]
        stage[0, 0, j] = fwd
        after = lam * fwd + pair[0, 0, j]
        stage[1, 0, j] = after
        stage[1, 1, j] = bwd
        stage[0, 1, j] = lam * bwd + pair[1, 1, j]
        farb[j] = pair[0, 1, j] * fwd + pair[1, 1, j] * after
    last = remote(stage.at[other], ent_ref.at[core], ent_s, ent_r, (ctx, other))
    last.start()
    ent_ref[core] = stage[core]

    owned, poles, width = farb.shape[1:]
    far = farb[...].reshape(q_n * owned * poles, width).T
    far = jnp.sum(far, axis=0, keepdims=True)
    resb[ctx] = npair[0] + npair[1] + scale_ref[0, core] * far
    res_copies = []
    for k in range(1, n_ctx):
        to = (ctx + k) % n_ctx
        copy = remote(resb.at[ctx], resb.at[ctx], res_s.at[to], res_r.at[ctx], (to, core))
        copy.start()
        res_copies.append(copy)
    for k in range(1, n_ctx):
        src = (ctx + k) % n_ctx
        remote(resb.at[src], resb.at[src], res_s.at[src], res_r.at[src], (src, core)).wait_recv()
    total = resb[0]
    for j in range(1, n_ctx):
        total = total + resb[j]
    res_ref[...] = scale_ref[1, core] * total
    last.wait()
    for copy in plane_copies + zed_copies + back_copies + res_copies:
        copy.wait_send()


def conv_kernel(
    group, width, poles, q_ref, k_ref, v_ref, c_ref, pc_ref, pr_ref, e_ref,
    mixed_ref, gq_ref, gk_ref, gv_ref,
):
    rows = q_ref.shape[0]
    place_l = lax.broadcasted_iota(jnp.int32, (poles, rows), 1).astype(F32)
    place_s = lax.broadcasted_iota(jnp.int32, (rows, 3 * poles), 0).astype(F32)
    lane = lax.broadcasted_iota(jnp.int32, (rows, 3 * poles), 1)
    middle = (lane >= poles) & (lane < 2 * poles)
    row_id = lax.broadcasted_iota(jnp.int32, (rows, rows), 0)
    col_id = lax.broadcasted_iota(jnp.int32, (rows, rows), 1)

    def left(x):
        high = x.astype(BF16).astype(F32)
        return jnp.where(middle, x - high, high).astype(BF16)

    def right(x):
        high, low = split(x)
        return jnp.concatenate([high, high, low], axis=0)

    def convolve(a, table, state, keep, hi, lo):
        wide = mm(a, lanes(right(state), right(table)))
        th, tl = split(jnp.where(keep, wide[:, width:], 0.0))
        inner = mm(th, lanes(hi, lo))
        return (inner[:, :width] + wide[:, :width]) + (inner[:, width:] + mm(tl, hi))

    for h in range(group):
        cols = slice(h * width, (h + 1) * width)
        rate = pc_ref[h, :, 0:1]
        coef = pc_ref[h, :, 1:2]
        step = pc_ref[h, :, 2:3]
        late = pc_ref[h, :, 3:4]
        rate_row = pr_ref[h, 0:1]
        coef_row = pr_ref[h, 1:2]
        query = q_ref[:, cols].astype(F32)
        key = k_ref[:, cols].astype(F32)
        value = v_ref[:, cols].astype(F32)
        cotan = c_ref[:, cols].astype(F32)
        ph, pl_ = split(key * value)
        gh, gl = split(cotan * query)
        decay_l = jnp.exp(-rate * place_l)
        growth_l = jnp.exp(rate * place_l)
        conv = convolve(
            left(coef_row * jnp.exp(-rate_row * place_s)),
            growth_l, step * e_ref[0, 0, h], row_id >= col_id, ph, pl_,
        )
        mixed_ref[:, cols] = (query * conv).astype(BF16)
        gq_ref[:, cols] = (cotan * conv).astype(BF16)
        gprod = convolve(
            left(jnp.exp(rate_row * place_s)),
            coef * decay_l, late * e_ref[0, 1, h], row_id <= col_id, gh, gl,
        )
        gk_ref[:, cols] = (gprod * value).astype(BF16)
        gv_ref[:, cols] = (gprod * key).astype(BF16)


def on_device(query, key_in, value, cotangent, decay_rate, residue):
    rows, features = query.shape
    heads, poles = decay_rate.shape
    width = features // heads
    n_ctx, cores = lax.axis_size("ctx"), lax.axis_size("head")
    half = heads // cores
    near_group = max(g for g in (1, 2, 4) if n_ctx % g == 0 and half % g == 0)
    owned = half // near_group
    group = max(g for g in (1, 2, 3, 4) if half % g == 0)
    per_half = half // group
    steps = heads // group

    norm = jnp.sqrt(-jnp.expm1(-2.0 * decay_rate))
    coef = residue * norm
    one = jnp.exp(-decay_rate)
    late = coef * jnp.exp(-decay_rate * rows)
    pc = jnp.stack([decay_rate, coef, one, late], axis=-1)
    pr = jnp.tile(jnp.stack([decay_rate, coef], axis=1), (1, 1, 3))
    spans = jnp.array([1.0, cores, cores * near_group], F32) * rows
    lam = jnp.exp(-spans[:, None, None] * decay_rate[None])
    lam = lam.reshape(3, cores, near_group, owned, poles, 1)
    total_rows = rows * n_ctx * cores
    scale = jnp.stack([one, norm / math.sqrt(float(total_rows * width))])
    scale = scale.reshape(2, cores, 1, half * poles)

    big = pl.BlockSpec((rows, group * width), lambda g: (0, g))
    pc_spec = pl.BlockSpec((group, poles, 4), lambda g: (g, 0, 0))
    pr_spec = pl.BlockSpec((group, 2, 3 * poles), lambda g: (g, 0, 0))
    state_spec = pl.BlockSpec(
        (1, 2, group, poles, width), lambda g: (g // per_half, 0, g % per_half, 0, 0)
    )
    state_shape = jax.ShapeDtypeStruct((cores, 2, half, poles, width), F32)
    limit = 32 * 2**20
    flops = 2 * heads * rows * rows * width
    area = rows * features * 2

    states, near = pl.pallas_call(
        functools.partial(state_kernel, group, width, poles),
        grid=(steps,),
        in_specs=[big] * 4 + [pc_spec, pr_spec],
        out_specs=[state_spec, pl.BlockSpec((group, 1, poles), lambda g: (g, 0, 0))],
        out_shape=[state_shape, jax.ShapeDtypeStruct((heads, 1, poles), F32)],
        compiler_params=pltpu.CompilerParams(vmem_limit_bytes=limit),
        cost_estimate=pl.CostEstimate(
            flops=5 * flops, bytes_accessed=4 * area, transcendentals=0
        ),
        name="states",
    )(query, key_in, value, cotangent, pc, pr)

    in_vmem = pl.BlockSpec(memory_space=pltpu.VMEM)
    part = (owned, poles, width)
    sem = pltpu.SemaphoreType.DMA
    z_n = n_ctx // near_group
    entering, res = pl.pallas_call(
        functools.partial(chain_kernel, near_group),
        in_specs=[in_vmem] * 4,
        out_specs=[in_vmem] * 2,
        out_shape=[
            jax.ShapeDtypeStruct((cores, 2, near_group) + part, F32),
            jax.ShapeDtypeStruct((1, half * poles), F32),
        ],
        scratch_shapes=[
            pltpu.VMEM((cores, 2, near_group) + part, F32),
            pltpu.VMEM((cores, 1, half * poles), F32),
            pltpu.VMEM((near_group, 2) + part, F32),
            pltpu.VMEM((near_group, 2) + part, F32),
            pltpu.VMEM((2,) + part, F32),
            pltpu.VMEM((z_n,) + part, F32),
            pltpu.VMEM((near_group, 2) + part, F32),
            pltpu.VMEM((near_group, 2) + part, F32),
            pltpu.VMEM((cores, 2, near_group) + part, F32),
            pltpu.VMEM((near_group,) + part, F32),
            pltpu.VMEM((n_ctx, 1, half * poles), F32),
            sem((2,)), sem((2,)),
            sem((near_group,)), sem((near_group,)),
            sem((z_n,)), sem((z_n,)),
            sem((near_group,)), sem((near_group,)),
            sem, sem,
            sem((n_ctx,)), sem((n_ctx,)),
        ],
        compiler_params=pltpu.CompilerParams(
            collective_id=0, has_side_effects=True, vmem_limit_bytes=limit
        ),
        name="chain",
    )(
        states.reshape((cores, 2, near_group) + part),
        near.reshape(cores, 1, half * poles), lam, scale,
    )

    outs = pl.pallas_call(
        functools.partial(conv_kernel, group, width, poles),
        grid=(steps,),
        in_specs=[big] * 4 + [pc_spec, pr_spec, state_spec],
        out_specs=[big] * 4,
        out_shape=[jax.ShapeDtypeStruct((rows, features), BF16)] * 4,
        compiler_params=pltpu.CompilerParams(vmem_limit_bytes=limit),
        cost_estimate=pl.CostEstimate(
            flops=8 * flops, bytes_accessed=8 * area, transcendentals=0
        ),
        name="convolve",
    )(
        query, key_in, value, cotangent, pc, pr,
        entering.reshape(cores, 2, half, poles, width),
    )
    return (*outs, res.reshape(half, poles))


def solution(mesh):
    wide = P(("ctx", "head"), None)
    return jax.shard_map(
        on_device,
        mesh=mesh,
        in_specs=(wide, wide, wide, wide, P(), P()),
        out_specs=(wide, wide, wide, wide, P("head", None)),
        check_vma=False,
    )
```

time: 377 us -> 100 us (0.27); the launches traced: 371 us -> 99.5 us
  blocking collectives: 119 us -> 0 us
  matrix products: 102 us -> 0 us
  Pallas kernels: 0 us -> 69.7 us
  waiting for transfers between devices: 54.2 us -> 0 us
  other arithmetic: 47.8 us -> 6.7 us
  between operations: 14.9 us -> 0.72 us
  local copies, waits for them, and re-layouts: 31 us -> 22.3 us
    dot_general x9 -> x0, matrix products: 102 us -> none  [the longest x1 22.2 us: modal_layer(): jnp.einsum('hij,bihc->bjhc', toeplitz, grad_conv, precision=HIGHEST)]
    psum x1 -> x0, blocking collectives: 74.1 us -> none  [on_device(): summed = lax.psum(results[4], ('ctx', 'head'))]
    pallas_call x0 -> x3, Pallas kernels: none -> 69.7 us  [the longest x1 31.7 us: on_device(): pl.pallas_call(functools.partial(chain_kernel, near_group), in_specs=[in_...]
    all_gather x2 -> x0, waiting for transfers between devices: 54.2 us -> none  [entering_2(): gathered = jax.tree.map(lambda a: lax.all_gather(a, axis), part)]
    all_gather x1 -> x0, blocking collectives: 44.7 us -> none  [entering_2(): gathered = jax.tree.map(lambda a: lax.all_gather(a, axis), part)]
    add x32 -> x0, other arithmetic: 37.5 us -> none  [the longest x31 36.6 us: combine_states(): later_part[0][..., None] * earlier[1] + later_part[1]]
    unnamed x8 -> x0, other arithmetic: 9.59 us -> none
    unnamed x56 -> x24, local copies, waits for them, and re-layouts: 24.3 us -> 14.9 us
  transfers between devices with their start and end apart: 2 -> 0, of which waited for: 1 -> 0; matrix products, arithmetic and copies ran while one was open for 27% -> 0% of each run, Pallas kernels for 0% -> 0%
where the time goes in v1:
time: 100 us; the launch traced here: 99.5 us
  Pallas kernels  69.7 us (70%)
  local copies, waits for them, and re-layouts  22.3 us (22%)
  other arithmetic  6.7 us (7%)
    pallas_call x1, Pallas kernels, on_device(): pl.pallas_call(functools.partial(chain_kernel, near_group), in_specs=[in_...  31.7 us
    pallas_call x1, Pallas kernels, on_device(): pl.pallas_call(functools.partial(conv_kernel, group, width, poles), grid=...  22.9 us
    pallas_call x1, Pallas kernels, on_device(): pl.pallas_call(functools.partial(state_kernel, group, width, poles), grid...  15.1 us
    unnamed x24, local copies, waits for them, and re-layouts  14.9 us
    pallas_call x1, other arithmetic, on_device(): pl.pallas_call(functools.partial(state_kernel, group, width, poles), grid...  2.25 us
    another operation x2, local copies, waits for them, and re-layouts, on_device(): scale = jnp.stack([one, norm / math.sqrt(float(total_rows * width))])  2.22 us

profile of v1, /device:TPU:0, one launch (start us, length us, event | category | flops | bytes accessed | tf_op | source)
XLA Modules:
  0.0 99.5 jit_solution(6277172317242320314)
XLA Ops:
  0.6 1.3 %negate_exponential_fusion = (f32[48,16]{0,1:T(8,128)}, f32[48,16,1]{0,1,2:T(8,128)S(1)}, f32[48,16,1]{0,1,2:T(8,128)S(1)}, f32[48,16,1]{0,1,2:T(8,128)S(1)}, f32[48,1,16]{0,2,1:T(8,128)S(1)}, /*index=5*/f32[48,16]{0,1:T(8,128)S(1)}) fusion(f32[48,16]{0,1:T(8,128)} %param.11, f32[48,16]{0,1:T(8,128)} %param.12), kind=kLoop, calls=%fused_computation.5 | loop fusion | flops 5376 | bytes 24576 | tf_op jit(solution)/shard_map/exp | solution.py:277
  2.0 0.7 pad_maximum_fusion
  2.9 0.7 pad_maximum_fusion.1
  3.7 1.7 %copy-done = bf16[192,6144]{1,0:T(8,128)(2,1)S(1)} copy-done((bf16[192,6144]{1,0:T(8,128)(2,1)S(1)}, bf16[192,6144]{1,0:T(8,128)(2,1)}, u32[]{:S(2)}) %copy-start) | copy-done | bytes 2359320
  5.4 1.7 %copy-done.2 = bf16[192,6144]{1,0:T(8,128)(2,1)S(1)} copy-done((bf16[192,6144]{1,0:T(8,128)(2,1)S(1)}, bf16[192,6144]{1,0:T(8,128)(2,1)}, u32[]{:S(2)}) %copy-start.2) | copy-done | bytes 2359320
  7.1 1.7 %copy-done.4 = bf16[192,6144]{1,0:T(8,128)(2,1)S(1)} copy-done((bf16[192,6144]{1,0:T(8,128)(2,1)S(1)}, bf16[192,6144]{1,0:T(8,128)(2,1)}, u32[]{:S(2)}) %copy-start.4) | copy-done | bytes 2359320
  8.7 1.7 %copy-done.6 = bf16[192,6144]{1,0:T(8,128)(2,1)S(1)} copy-done((bf16[192,6144]{1,0:T(8,128)(2,1)S(1)}, bf16[192,6144]{1,0:T(8,128)(2,1)}, u32[]{:S(2)}) %copy-start.6) | copy-done | bytes 2359320
  10.4 15.1 %states.1 = (f32[2,2,24,16,128]{4,3,2,1,0:T(8,128)S(1)}, f32[48,1,16]{2,1,0:T(1,128)S(1)}) custom-call(bf16[192,6144]{1,0:T(8,128)(2,1)S(1)} %copy-done, bf16[192,6144]{1,0:T(8,128)(2,1)S(1)} %copy-done.2, bf16[192,6144]{1,0:T(8,128)(2,1)S(1)} %copy-done.4, bf16[192,6144]{1,0:T(8,128)(2,1)S(1)} %copy-done.6, f32[48,16,4]{2,1,0:T(8,128)S(1)} %copy.78.pc_ref, ...), custom_call_target="tpu_custom_call" | custom-call | flops 2264924160 | bytes 9437184 | tf_op jit(solution)/shard_map/states/pallas_call | solution.py:299
  27.3 2.2 %reduce.4 = f32[48,16]{1,0:T(8,128)} reduce(f32[48,1,16]{2,1,0:T(1,128)} %copy-done.10, f32[]{:T(128)} %broadcast.27), dimensions={1}, to_apply=%get-tuple-element.14.reduce_sub_computation.3 | reduce | bytes 6148 | tf_op jit(solution)/shard_map/states/pallas_call | solution.py:299
  29.5 0.8 reshape.47.near_ref
  30.3 1.4 %copy.73 = f32[48,16]{1,0:T(8,128)} copy(f32[48,16]{0,1:T(8,128)} %get-tuple-element.49) | data formatting | bytes 6144 | tf_op jit(solution)/shard_map/exp | solution.py:277
  31.7 1.4 %stack.44 = f32[1,2,1,384]{3,2,1,0:T(1,128)} reshape(f32[48,16]{1,0:T(8,128)} %copy.73) | data formatting | bytes 6144 | tf_op jit(solution)/shard_map/stack | solution.py:285
  33.1 0.7 copy.74
  33.8 0.8 stack.45
  34.6 0.7 pad_maximum_fusion.2.scale_ref
  35.3 1.4 %copy.72 = f32[48,16]{1,0:T(8,128)} copy(f32[48,16]{0,1:T(8,128)} %param.11) | data formatting | bytes 6144 | tf_op args[4]
  36.7 1.4 %mul.51 = f32[2,4,6,16]{3,2,1,0:T(8,128)} reshape(f32[48,16]{1,0:T(8,128)} %copy.72) | data formatting | bytes 6144 | tf_op jit(solution)/shard_map/mul | solution.py:282
  38.1 1.0 %multiply_exponential_fusion.lam_ref = f32[3,2,4,6,16,1]{5,4,3,2,1,0:T(8,128)S(1)} fusion(f32[2,4,6,16]{3,2,1,0:T(8,128)} %mul.51, f32[3]{0:T(128)} %constant.12), kind=kLoop, calls=%fused_computation | loop fusion | flops 2304 | bytes 12300 | tf_op jit(solution)/shard_map/exp | solution.py:282
  39.1 31.7 %chain.1 = (f32[2,2,4,6,16,128]{5,4,3,2,1,0:T(8,128)S(1)}, f32[1,384]{1,0:T(1,128)S(1)}) custom-call(f32[2,2,4,6,16,128]{5,4,3,2,1,0:T(8,128)S(1)} %bitcast.13, f32[2,1,384]{2,1,0:T(1,128)S(1)} %reshape.47.near_ref, f32[3,2,4,6,16,1]{5,4,3,2,1,0:T(8,128)S(1)} %multiply_exponential_fusion.lam_ref, f32[2,2,1,384]{3,2,1,0:T(1,128)S(1)} %pad_maximum_fusion.2.scale_ref), custom_call_target="tpu_custom_call" | custom-call | tf_op jit(solution)/shard_map/chain/pallas_call | solution.py:316
  70.8 1.7 %copy-done.3 = bf16[192,6144]{1,0:T(8,128)(2,1)S(1)} copy-done((bf16[192,6144]{1,0:T(8,128)(2,1)S(1)}, bf16[192,6144]{1,0:T(8,128)(2,1)}, u32[]{:S(2)}) %copy-start.3) | copy-done | bytes 2359320
  72.5 1.7 %copy-done.5 = bf16[192,6144]{1,0:T(8,128)(2,1)S(1)} copy-done((bf16[192,6144]{1,0:T(8,128)(2,1)S(1)}, bf16[192,6144]{1,0:T(8,128)(2,1)}, u32[]{:S(2)}) %copy-start.5) | copy-done | bytes 2359320
  74.1 1.7 %copy-done.7 = bf16[192,6144]{1,0:T(8,128)(2,1)S(1)} copy-done((bf16[192,6144]{1,0:T(8,128)(2,1)S(1)}, bf16[192,6144]{1,0:T(8,128)(2,1)}, u32[]{:S(2)}) %copy-start.7) | copy-done | bytes 2359320
  75.8 22.9 %convolve.1 = (bf16[192,6144]{1,0:T(8,128)(2,1)}, bf16[192,6144]{1,0:T(8,128)(2,1)}, bf16[192,6144]{1,0:T(8,128)(2,1)}, bf16[192,6144]{1,0:T(8,128)(2,1)}) custom-call(bf16[192,6144]{1,0:T(8,128)(2,1)S(1)} %copy-done.1, bf16[192,6144]{1,0:T(8,128)(2,1)S(1)} %copy-done.3, bf16[192,6144]{1,0:T(8,128)(2,1)S(1)} %copy-done.5, bf16[192,6144]{1,0:T(8,128)(2,1)S(1)} %copy-done.7, ...), custom_call_target="tpu_custom_call" | custom-call | flops 3623878656 | bytes 18874368 | tf_op jit(solution)/shard_map/convolve/pallas_call | solution.py:352
  98.8 0.7 copy.80
  (21 shorter events, 2.2 us)
Async XLA Ops:
  3.7 1.7 %copy-start = (bf16[192,6144]{1,0:T(8,128)(2,1)S(1)}, bf16[192,6144]{1,0:T(8,128)(2,1)}, u32[]{:S(2)}) copy-start(bf16[192,6144]{1,0:T(8,128)(2,1)} %q_ref.3) | copy-start | bytes 7077892
  5.4 1.7 %copy-start.2 = (bf16[192,6144]{1,0:T(8,128)(2,1)S(1)}, bf16[192,6144]{1,0:T(8,128)(2,1)}, u32[]{:S(2)}) copy-start(bf16[192,6144]{1,0:T(8,128)(2,1)} %k_ref.3) | copy-start | bytes 7077892
  7.1 1.7 %copy-start.4 = (bf16[192,6144]{1,0:T(8,128)(2,1)S(1)}, bf16[192,6144]{1,0:T(8,128)(2,1)}, u32[]{:S(2)}) copy-start(bf16[192,6144]{1,0:T(8,128)(2,1)} %v_ref.3) | copy-start | bytes 7077892
  8.7 1.7 %copy-start.6 = (bf16[192,6144]{1,0:T(8,128)(2,1)S(1)}, bf16[192,6144]{1,0:T(8,128)(2,1)}, u32[]{:S(2)}) copy-start(bf16[192,6144]{1,0:T(8,128)(2,1)} %c_ref.3) | copy-start | bytes 7077892
  25.5 0.6 copy-start.8
  26.1 0.6 copy-start.10
  26.8 44.0 %copy-start.1 = (bf16[192,6144]{1,0:T(8,128)(2,1)S(1)}, bf16[192,6144]{1,0:T(8,128)(2,1)}, u32[]{:S(2)}) copy-start(bf16[192,6144]{1,0:T(8,128)(2,1)} %q_ref.3) | copy-start | bytes 7077892
  38.1 32.7 %copy-start.9 = (f32[48,2,48]{2,1,0:T(2,128)S(1)}, f32[48,2,48]{2,1,0:T(2,128)}, u32[]{:S(2)}) copy-start(f32[48,2,48]{2,1,0:T(2,128)} %copy-done.8) | copy-start | bytes 55300
  70.8 1.7 %copy-start.3 = (bf16[192,6144]{1,0:T(8,128)(2,1)S(1)}, bf16[192,6144]{1,0:T(8,128)(2,1)}, u32[]{:S(2)}) copy-start(bf16[192,6144]{1,0:T(8,128)(2,1)} %k_ref.3) | copy-start | bytes 7077892
  72.5 1.7 %copy-start.5 = (bf16[192,6144]{1,0:T(8,128)(2,1)S(1)}, bf16[192,6144]{1,0:T(8,128)(2,1)}, u32[]{:S(2)}) copy-start(bf16[192,6144]{1,0:T(8,128)(2,1)} %v_ref.3) | copy-start | bytes 7077892
  74.1 1.7 %copy-start.7 = (bf16[192,6144]{1,0:T(8,128)(2,1)S(1)}, bf16[192,6144]{1,0:T(8,128)(2,1)}, u32[]{:S(2)}) copy-start(bf16[192,6144]{1,0:T(8,128)(2,1)} %c_ref.3) | copy-start | bytes 7077892

commit v2 on v1

--- a/solution.py
+++ b/solution.py
@@ -26,11 +26,22 @@
     return lax.dot_general(a, b, LAST, preferred_element_type=F32)
 
 
+def column(row):
+    count = row.shape[1]
+    same = lax.broadcasted_iota(jnp.int32, (count, count), 0) == lax.broadcasted_iota(
+        jnp.int32, (count, count), 1
+    )
+    return jnp.sum(jnp.where(same, row, 0.0), axis=1, keepdims=True)
+
+
 def lanes(a, b):
     return jnp.concatenate([a, b], axis=1)
 
 
-def state_kernel(group, width, poles, q_ref, k_ref, v_ref, c_ref, pc_ref, pr_ref, s_ref, near_ref):
+def state_kernel(
+    group, width, poles, share, q_ref, k_ref, v_ref, c_ref, rate_ref, norm_ref,
+    s_ref, near_ref, par_ref,
+):
     rows = q_ref.shape[0]
     place_l = lax.broadcasted_iota(jnp.int32, (poles, rows), 1).astype(F32)
     place_s = lax.broadcasted_iota(jnp.int32, (rows, poles), 0).astype(F32)
@@ -39,8 +50,12 @@
     )
     for h in range(group):
         cols = slice(h * width, (h + 1) * width)
-        rate = pc_ref[h, :, 0:1]
-        rate_row = pr_ref[h, 0:1, :poles]
+        rate_row = rate_ref[h : h + 1, :]
+        norm_row = norm_ref[h : h + 1, :] * share
+        rate = column(rate_row)
+        far_scale = column(norm_row * jnp.exp(-rate_row))
+        lane = lax.broadcasted_iota(jnp.int32, (poles, width), 1)
+        par_ref[0, h] = jnp.where(lane == 0, rate, far_scale)
         ph, pl_ = split(k_ref[:, cols].astype(F32) * v_ref[:, cols].astype(F32))
         gh, gl = split(c_ref[:, cols].astype(F32) * q_ref[:, cols].astype(F32))
         for d, (hi, lo, lag) in enumerate(
@@ -55,11 +70,12 @@
         wh, wl = split(jnp.exp(rate * place_l))
         grown = mm_t(xh, jnp.concatenate([wh, wl], axis=0))
         grown = grown[:, :poles] + grown[:, poles:] + mm_t(xl, wh)
-        near_ref[h] = jnp.sum(grown * jnp.exp(-rate_row * place_s), axis=0, keepdims=True)
+        near = jnp.sum(grown * jnp.exp(-rate_row * place_s), axis=0, keepdims=True)
+        near_ref[h : h + 1, :] = norm_row * near
 
 
 def chain_kernel(
-    near_group, s_ref, near_ref, lam_ref, scale_ref, ent_ref, res_ref,
+    near_group, rows, s_ref, near_ref, par_ref, ent_ref, res_ref,
     pair, npair, chip, plane, tot, zed, back, got, stage, farb, resb,
     pair_s, pair_r, plane_s, plane_r, zed_s, zed_r, back_s, back_r, ent_s, ent_r, res_s, res_r,
 ):
@@ -78,6 +94,9 @@
             device_id=where, device_id_type=pl.DeviceIdType.MESH,
         )
 
+    def decay(slot, count):
+        return jnp.exp(par_ref[core, slot, :, :, 0:1] * (-float(rows * count)))
+
     barrier = pltpu.get_barrier_semaphore()
     pl.semaphore_signal(
         barrier, inc=1, device_id=(ctx, other), device_id_type=pl.DeviceIdType.MESH
@@ -103,7 +122,7 @@
     plane_copies = []
     for k in range(1, q_n + 1):
         to = (q + k) % q_n
-        lam = lam_ref[0, core, to]
+        lam = decay(to, 1)
         chip[to, 0] = lam * pair[0, 0, to] + pair[1, 0, to]
         chip[to, 1] = pair[0, 1, to] + lam * pair[1, 1, to]
         if k < q_n:
@@ -118,7 +137,7 @@
         remote(
             chip.at[src], plane.at[src], plane_s.at[src], plane_r.at[src], (z * q_n + src, core)
         ).wait_recv()
-    lam2 = lam_ref[1, core, q]
+    lam2 = decay(q, 2)
     fwd = plane[0, 0]
     bwd = plane[q_n - 1, 1]
     for j in range(1, q_n):
@@ -141,7 +160,7 @@
         remote(
             tot.at[0], zed.at[src], zed_s.at[src], zed_r.at[src], (src * q_n + q, core)
         ).wait_recv()
-    lam3 = lam_ref[2, core, q]
+    lam3 = decay(q, 2 * q_n)
     fwd = jnp.zeros_like(fwd)
     bwd = jnp.zeros_like(bwd)
     for j in range(z_n):
@@ -169,7 +188,7 @@
         ).wait_recv()
 
     for j in range(q_n):
-        lam = lam_ref[0, core, j]
+        lam = decay(j, 1)
         fwd = got[j, 0]
         bwd = got[j, 1]
         stage[0, 0, j] = fwd
@@ -177,15 +196,14 @@
         stage[1, 0, j] = after
         stage[1, 1, j] = bwd
         stage[0, 1, j] = lam * bwd + pair[1, 1, j]
-        farb[j] = pair[0, 1, j] * fwd + pair[1, 1, j] * after
+        farb[j] = par_ref[core, j, :, :, 1:2] * (pair[0, 1, j] * fwd + pair[1, 1, j] * after)
     last = remote(stage.at[other], ent_ref.at[core], ent_s, ent_r, (ctx, other))
     last.start()
     ent_ref[core] = stage[core]
 
     owned, poles, width = farb.shape[1:]
-    far = farb[...].reshape(q_n * owned * poles, width).T
-    far = jnp.sum(far, axis=0, keepdims=True)
-    resb[ctx] = npair[0] + npair[1] + scale_ref[0, core] * far
+    far = jnp.sum(farb[...].reshape(q_n * owned, poles, width), axis=-1)
+    resb[ctx] = npair[0] + npair[1] + far
     res_copies = []
     for k in range(1, n_ctx):
         to = (ctx + k) % n_ctx
@@ -198,14 +216,14 @@
     total = resb[0]
     for j in range(1, n_ctx):
         total = total + resb[j]
-    res_ref[...] = scale_ref[1, core] * total
+    res_ref[...] = total
     last.wait()
     for copy in plane_copies + zed_copies + back_copies + res_copies:
         copy.wait_send()
 
 
 def conv_kernel(
-    group, width, poles, q_ref, k_ref, v_ref, c_ref, pc_ref, pr_ref, e_ref,
+    group, width, poles, q_ref, k_ref, v_ref, c_ref, rate_ref, norm_ref, residue_ref, e_ref,
     mixed_ref, gq_ref, gk_ref, gv_ref,
 ):
     rows = q_ref.shape[0]
@@ -213,6 +231,9 @@
     place_s = lax.broadcasted_iota(jnp.int32, (rows, 3 * poles), 0).astype(F32)
     lane = lax.broadcasted_iota(jnp.int32, (rows, 3 * poles), 1)
     middle = (lane >= poles) & (lane < 2 * poles)
+    tiled = lax.broadcasted_iota(jnp.int32, (poles, 3 * poles), 0) == lax.rem(
+        lax.broadcasted_iota(jnp.int32, (poles, 3 * poles), 1), poles
+    )
     row_id = lax.broadcasted_iota(jnp.int32, (rows, rows), 0)
     col_id = lax.broadcasted_iota(jnp.int32, (rows, rows), 1)
 
@@ -232,12 +253,12 @@
 
     for h in range(group):
         cols = slice(h * width, (h + 1) * width)
-        rate = pc_ref[h, :, 0:1]
-        coef = pc_ref[h, :, 1:2]
-        step = pc_ref[h, :, 2:3]
-        late = pc_ref[h, :, 3:4]
-        rate_row = pr_ref[h, 0:1]
-        coef_row = pr_ref[h, 1:2]
+        rate = column(rate_ref[h : h + 1, :])
+        coef = column(norm_ref[h : h + 1, :] * residue_ref[h : h + 1, :])
+        step = jnp.exp(-rate)
+        late = coef * jnp.exp(rate * (-float(rows)))
+        rate_row = jnp.sum(jnp.where(tiled, rate, 0.0), axis=0, keepdims=True)
+        coef_row = jnp.sum(jnp.where(tiled, coef, 0.0), axis=0, keepdims=True)
         query = q_ref[:, cols].astype(F32)
         key = k_ref[:, cols].astype(F32)
         value = v_ref[:, cols].astype(F32)
@@ -268,62 +289,61 @@
     half = heads // cores
     near_group = max(g for g in (1, 2, 4) if n_ctx % g == 0 and half % g == 0)
     owned = half // near_group
-    group = max(g for g in (1, 2, 3, 4) if half % g == 0)
+    group = 8 if half % 8 == 0 else half
     per_half = half // group
     steps = heads // group
 
     norm = jnp.sqrt(-jnp.expm1(-2.0 * decay_rate))
-    coef = residue * norm
-    one = jnp.exp(-decay_rate)
-    late = coef * jnp.exp(-decay_rate * rows)
-    pc = jnp.stack([decay_rate, coef, one, late], axis=-1)
-    pr = jnp.tile(jnp.stack([decay_rate, coef], axis=1), (1, 1, 3))
-    spans = jnp.array([1.0, cores, cores * near_group], F32) * rows
-    lam = jnp.exp(-spans[:, None, None] * decay_rate[None])
-    lam = lam.reshape(3, cores, near_group, owned, poles, 1)
-    total_rows = rows * n_ctx * cores
-    scale = jnp.stack([one, norm / math.sqrt(float(total_rows * width))])
-    scale = scale.reshape(2, cores, 1, half * poles)
+    share = 1.0 / math.sqrt(float(rows * n_ctx * cores * width))
 
     big = pl.BlockSpec((rows, group * width), lambda g: (0, g))
-    pc_spec = pl.BlockSpec((group, poles, 4), lambda g: (g, 0, 0))
-    pr_spec = pl.BlockSpec((group, 2, 3 * poles), lambda g: (g, 0, 0))
+    par_spec = pl.BlockSpec((group, poles), lambda g: (g, 0))
     state_spec = pl.BlockSpec(
         (1, 2, group, poles, width), lambda g: (g // per_half, 0, g % per_half, 0, 0)
     )
     state_shape = jax.ShapeDtypeStruct((cores, 2, half, poles, width), F32)
-    limit = 32 * 2**20
+    limit = 60 * 2**20
     flops = 2 * heads * rows * rows * width
     area = rows * features * 2
 
-    states, near = pl.pallas_call(
-        functools.partial(state_kernel, group, width, poles),
+    states, near, par = pl.pallas_call(
+        functools.partial(state_kernel, group, width, poles, share),
         grid=(steps,),
-        in_specs=[big] * 4 + [pc_spec, pr_spec],
-        out_specs=[state_spec, pl.BlockSpec((group, 1, poles), lambda g: (g, 0, 0))],
-        out_shape=[state_shape, jax.ShapeDtypeStruct((heads, 1, poles), F32)],
+        in_specs=[big] * 4 + [par_spec] * 2,
+        out_specs=[
+            state_spec,
+            par_spec,
+            pl.BlockSpec(
+                (1, group, poles, width), lambda g: (g // per_half, g % per_half, 0, 0)
+            ),
+        ],
+        out_shape=[
+            state_shape,
+            jax.ShapeDtypeStruct((heads, poles), F32),
+            jax.ShapeDtypeStruct((cores, half, poles, width), F32),
+        ],
         compiler_params=pltpu.CompilerParams(vmem_limit_bytes=limit),
         cost_estimate=pl.CostEstimate(
             flops=5 * flops, bytes_accessed=4 * area, transcendentals=0
         ),
         name="states",
-    )(query, key_in, value, cotangent, pc, pr)
+    )(query, key_in, value, cotangent, decay_rate, norm)
 
     in_vmem = pl.BlockSpec(memory_space=pltpu.VMEM)
     part = (owned, poles, width)
     sem = pltpu.SemaphoreType.DMA
     z_n = n_ctx // near_group
     entering, res = pl.pallas_call(
-        functools.partial(chain_kernel, near_group),
-        in_specs=[in_vmem] * 4,
+        functools.partial(chain_kernel, near_group, rows),
+        in_specs=[in_vmem] * 3,
         out_specs=[in_vmem] * 2,
         out_shape=[
             jax.ShapeDtypeStruct((cores, 2, near_group) + part, F32),
-            jax.ShapeDtypeStruct((1, half * poles), F32),
+            jax.ShapeDtypeStruct((half, poles), F32),
         ],
         scratch_shapes=[
             pltpu.VMEM((cores, 2, near_group) + part, F32),
-            pltpu.VMEM((cores, 1, half * poles), F32),
+            pltpu.VMEM((cores, half, poles), F32),
             pltpu.VMEM((near_group, 2) + part, F32),
             pltpu.VMEM((near_group, 2) + part, F32),
             pltpu.VMEM((2,) + part, F32),
@@ -332,7 +352,7 @@
             pltpu.VMEM((near_group, 2) + part, F32),
             pltpu.VMEM((cores, 2, near_group) + part, F32),
             pltpu.VMEM((near_group,) + part, F32),
-            pltpu.VMEM((n_ctx, 1, half * poles), F32),
+            pltpu.VMEM((n_ctx, half, poles), F32),
             sem((2,)), sem((2,)),
             sem((near_group,)), sem((near_group,)),
             sem((z_n,)), sem((z_n,)),
@@ -346,13 +366,13 @@
         name="chain",
     )(
         states.reshape((cores, 2, near_group) + part),
-        near.reshape(cores, 1, half * poles), lam, scale,
+        near.reshape(cores, half, poles), par.reshape((cores, near_group) + part),
     )
 
     outs = pl.pallas_call(
         functools.partial(conv_kernel, group, width, poles),
         grid=(steps,),
-        in_specs=[big] * 4 + [pc_spec, pr_spec, state_spec],
+        in_specs=[big] * 4 + [par_spec] * 3 + [state_spec],
         out_specs=[big] * 4,
         out_shape=[jax.ShapeDtypeStruct((rows, features), BF16)] * 4,
         compiler_params=pltpu.CompilerParams(vmem_limit_bytes=limit),
@@ -361,10 +381,10 @@
         ),
         name="convolve",
     )(
-        query, key_in, value, cotangent, pc, pr,
+        query, key_in, value, cotangent, decay_rate, norm, residue,
         entering.reshape(cores, 2, half, poles, width),
     )
-    return (*outs, res.reshape(half, poles))
+    return (*outs, res)
 
 
 def solution(mesh):

time: 100 us -> 77.4 us (0.77)
  local copies, waits for them, and re-layouts: 22.3 us -> 3.53 us
  other arithmetic: 6.7 us -> 0.63 us
  Pallas kernels: 69.7 us -> 72.2 us
    unnamed x24 -> x5, local copies, waits for them, and re-layouts: 14.9 us -> 3.53 us
    pallas_call x2, Pallas kernels: 46.8 us -> 49.6 us  [the longest x1 34.3 us: on_device(): pl.pallas_call(functools.partial(chain_kernel, near_group, rows), in_spec...]
    another operation x5 -> x0, local copies, waits for them, and re-layouts: 2.57 us -> none  [the longest x2 2.22 us: on_device(): scale = jnp.stack([one, norm / math.sqrt(float(total_rows * width))])]
    exp x2 -> x0, other arithmetic: 2.33 us -> none  [the longest x1 1.33 us: on_device(): one = jnp.exp(-decay_rate)]
    pallas_call x2 -> x0, other arithmetic: 2.27 us -> none  [the longest x1 2.25 us: on_device(): pl.pallas_call(functools.partial(state_kernel, group, width, poles), grid...]
    another operation x3 -> x0, other arithmetic: 2.1 us -> none  [the longest x1 0.7 us: on_device(): pr = jnp.tile(jnp.stack([decay_rate, coef], axis=1), (1, 1, 3))]
    exp x1 -> x0, local copies, waits for them, and re-layouts: 1.38 us -> none  [on_device(): one = jnp.exp(-decay_rate)]
    mul x1 -> x0, local copies, waits for them, and re-layouts: 1.35 us -> none  [on_device(): lam = jnp.exp(-spans[:, None, None] * decay_rate[None])]
where the time goes in v2:
time: 77.4 us; the launch traced here: 77 us
  Pallas kernels  72.2 us (93%)
  local copies, waits for them, and re-layouts  3.53 us (5%)
    pallas_call x1, Pallas kernels, on_device(): pl.pallas_call(functools.partial(chain_kernel, near_group, rows), in_spec...  34.3 us
    pallas_call x1, Pallas kernels, on_device(): pl.pallas_call(functools.partial(conv_kernel, group, width, poles), grid=...  22.6 us
    pallas_call x1, Pallas kernels, on_device(): pl.pallas_call(functools.partial(state_kernel, group, width, poles, share...  15.3 us
    unnamed x5, local copies, waits for them, and re-layouts  3.53 us

profile of v2, /device:TPU:0, one launch (start us, length us, event | category | flops | bytes accessed | tf_op | source)
XLA Modules:
  0.0 77.0 jit_solution(14986741302919762254)
XLA Ops:
  0.6 0.8 %copy.19.rate_ref = f32[48,16]{1,0:T(8,128)S(1)} copy(f32[48,16]{0,1:T(8,128)} %param.10) | data formatting | bytes 6144 | tf_op args[4]
  1.4 0.0 copy-start
  1.4 0.6 negate_sqrt_fusion.norm_ref
  2.0 1.4 %copy.20.residue_ref = f32[48,16]{1,0:T(8,128)} copy(f32[48,16]{0,1:T(8,128)} %param.11) | data formatting | bytes 6144 | tf_op args[5]
  3.4 0.0 copy-done
  3.4 15.3 %states.1 = (f32[2,2,24,16,128]{4,3,2,1,0:T(8,128)}, f32[48,16]{1,0:T(8,128)}, f32[2,24,16,128]{3,2,1,0:T(8,128)}) custom-call(bf16[192,6144]{1,0:T(8,128)(2,1)} %q_ref.3, bf16[192,6144]{1,0:T(8,128)(2,1)} %k_ref.3, bf16[192,6144]{1,0:T(8,128)(2,1)} %v_ref.3, bf16[192,6144]{1,0:T(8,128)(2,1)} %c_ref.3, f32[48,16]{1,0:T(8,128)} %copy-done, ...), custom_call_target="tpu_custom_call" | custom-call | flops 2264924160 | bytes 9437184 | tf_op jit(solution)/shard_map/states/pallas_call | solution.py:309
  18.8 34.3 %chain.1 = (f32[2,2,4,6,16,128]{5,4,3,2,1,0:T(8,128)}, f32[24,16]{1,0:T(8,128)}) custom-call(f32[2,2,4,6,16,128]{5,4,3,2,1,0:T(8,128)} %bitcast.4, f32[2,24,16]{2,1,0:T(8,128)} %bitcast.6, f32[2,4,6,16,128]{4,3,2,1,0:T(8,128)} %bitcast.5), custom_call_target="tpu_custom_call" | custom-call | tf_op jit(solution)/shard_map/chain/pallas_call | solution.py:336
  53.1 1.4 %copy.21 = f32[24,16]{0,1:T(8,128)} copy(f32[24,16]{1,0:T(8,128)} %get-tuple-element.32) | data formatting | bytes 3072
  54.4 22.6 %convolve.1 = (bf16[192,6144]{1,0:T(8,128)(2,1)}, bf16[192,6144]{1,0:T(8,128)(2,1)}, bf16[192,6144]{1,0:T(8,128)(2,1)}, bf16[192,6144]{1,0:T(8,128)(2,1)}) custom-call(bf16[192,6144]{1,0:T(8,128)(2,1)} %q_ref.3, bf16[192,6144]{1,0:T(8,128)(2,1)} %k_ref.3, bf16[192,6144]{1,0:T(8,128)(2,1)} %v_ref.3, bf16[192,6144]{1,0:T(8,128)(2,1)} %c_ref.3, ...), custom_call_target="tpu_custom_call" | custom-call | flops 3623878656 | bytes 18874368 | tf_op jit(solution)/shard_map/convolve/pallas_call | solution.py:372
Async XLA Ops:
  1.4 2.0 %copy-start = (f32[48,16]{1,0:T(8,128)}, f32[48,16]{1,0:T(8,128)S(1)}, u32[]{:S(2)}) copy-start(f32[48,16]{1,0:T(8,128)S(1)} %copy.19.rate_ref) | copy-start | bytes 9220

commit v3 on v2

--- a/solution.py
+++ b/solution.py
@@ -26,12 +26,18 @@
     return lax.dot_general(a, b, LAST, preferred_element_type=F32)
 
 
-def column(row):
-    count = row.shape[1]
-    same = lax.broadcasted_iota(jnp.int32, (count, count), 0) == lax.broadcasted_iota(
-        jnp.int32, (count, count), 1
-    )
-    return jnp.sum(jnp.where(same, row, 0.0), axis=1, keepdims=True)
+def pick(ref, place):
+    lane = lax.broadcasted_iota(jnp.int32, ref.shape, 1)
+    return jnp.sum(jnp.where(lane == place, ref[...], 0.0), axis=1, keepdims=True)
+
+
+def as_row(column, repeats):
+    count = column.shape[0]
+    shape = (count, repeats * count)
+    same = lax.broadcasted_iota(jnp.int32, shape, 0) == lax.rem(
+        lax.broadcasted_iota(jnp.int32, shape, 1), count
+    )
+    return jnp.sum(jnp.where(same, column, 0.0), axis=0, keepdims=True)
 
 
 def lanes(a, b):
@@ -43,6 +49,7 @@
     s_ref, near_ref, par_ref,
 ):
     rows = q_ref.shape[0]
+    first = pl.program_id(0) * group
     place_l = lax.broadcasted_iota(jnp.int32, (poles, rows), 1).astype(F32)
     place_s = lax.broadcasted_iota(jnp.int32, (rows, poles), 0).astype(F32)
     lower = lax.broadcasted_iota(jnp.int32, (rows, rows), 0) >= lax.broadcasted_iota(
@@ -50,10 +57,11 @@
     )
     for h in range(group):
         cols = slice(h * width, (h + 1) * width)
-        rate_row = rate_ref[h : h + 1, :]
-        norm_row = norm_ref[h : h + 1, :] * share
-        rate = column(rate_row)
-        far_scale = column(norm_row * jnp.exp(-rate_row))
+        rate = pick(rate_ref, first + h)
+        norm = pick(norm_ref, first + h) * share
+        rate_row = as_row(rate, 1)
+        norm_row = as_row(norm, 1)
+        far_scale = norm * jnp.exp(-rate)
         lane = lax.broadcasted_iota(jnp.int32, (poles, width), 1)
         par_ref[0, h] = jnp.where(lane == 0, rate, far_scale)
         ph, pl_ = split(k_ref[:, cols].astype(F32) * v_ref[:, cols].astype(F32))
@@ -216,7 +224,7 @@
     total = resb[0]
     for j in range(1, n_ctx):
         total = total + resb[j]
-    res_ref[...] = total
+    res_ref[...] = total.T
     last.wait()
     for copy in plane_copies + zed_copies + back_copies + res_copies:
         copy.wait_send()
@@ -227,13 +235,11 @@
     mixed_ref, gq_ref, gk_ref, gv_ref,
 ):
     rows = q_ref.shape[0]
+    first = pl.program_id(0) * group
     place_l = lax.broadcasted_iota(jnp.int32, (poles, rows), 1).astype(F32)
     place_s = lax.broadcasted_iota(jnp.int32, (rows, 3 * poles), 0).astype(F32)
     lane = lax.broadcasted_iota(jnp.int32, (rows, 3 * poles), 1)
     middle = (lane >= poles) & (lane < 2 * poles)
-    tiled = lax.broadcasted_iota(jnp.int32, (poles, 3 * poles), 0) == lax.rem(
-        lax.broadcasted_iota(jnp.int32, (poles, 3 * poles), 1), poles
-    )
     row_id = lax.broadcasted_iota(jnp.int32, (rows, rows), 0)
     col_id = lax.broadcasted_iota(jnp.int32, (rows, rows), 1)
 
@@ -253,12 +259,12 @@
 
     for h in range(group):
         cols = slice(h * width, (h + 1) * width)
-        rate = column(rate_ref[h : h + 1, :])
-        coef = column(norm_ref[h : h + 1, :] * residue_ref[h : h + 1, :])
+        rate = pick(rate_ref, first + h)
+        coef = pick(norm_ref, first + h) * pick(residue_ref, first + h)
         step = jnp.exp(-rate)
         late = coef * jnp.exp(rate * (-float(rows)))
-        rate_row = jnp.sum(jnp.where(tiled, rate, 0.0), axis=0, keepdims=True)
-        coef_row = jnp.sum(jnp.where(tiled, coef, 0.0), axis=0, keepdims=True)
+        rate_row = as_row(rate, 3)
+        coef_row = as_row(coef, 3)
         query = q_ref[:, cols].astype(F32)
         key = k_ref[:, cols].astype(F32)
         value = v_ref[:, cols].astype(F32)
@@ -293,11 +299,13 @@
     per_half = half // group
     steps = heads // group
 
-    norm = jnp.sqrt(-jnp.expm1(-2.0 * decay_rate))
+    rates, residues = decay_rate.T, residue.T
+    norm = jnp.sqrt(-jnp.expm1(-2.0 * rates))
     share = 1.0 / math.sqrt(float(rows * n_ctx * cores * width))
 
     big = pl.BlockSpec((rows, group * width), lambda g: (0, g))
     par_spec = pl.BlockSpec((group, poles), lambda g: (g, 0))
+    flat_spec = pl.BlockSpec((poles, heads), lambda g: (0, 0))
     state_spec = pl.BlockSpec(
         (1, 2, group, poles, width), lambda g: (g // per_half, 0, g % per_half, 0, 0)
     )
@@ -309,7 +317,7 @@
     states, near, par = pl.pallas_call(
         functools.partial(state_kernel, group, width, poles, share),
         grid=(steps,),
-        in_specs=[big] * 4 + [par_spec] * 2,
+        in_specs=[big] * 4 + [flat_spec] * 2,
         out_specs=[
             state_spec,
             par_spec,
@@ -327,7 +335,7 @@
             flops=5 * flops, bytes_accessed=4 * area, transcendentals=0
         ),
         name="states",
-    )(query, key_in, value, cotangent, decay_rate, norm)
+    )(query, key_in, value, cotangent, rates, norm)
 
     in_vmem = pl.BlockSpec(memory_space=pltpu.VMEM)
     part = (owned, poles, width)
@@ -339,7 +347,7 @@
         out_specs=[in_vmem] * 2,
         out_shape=[
             jax.ShapeDtypeStruct((cores, 2, near_group) + part, F32),
-            jax.ShapeDtypeStruct((half, poles), F32),
+            jax.ShapeDtypeStruct((poles, half), F32),
         ],
         scratch_shapes=[
             pltpu.VMEM((cores, 2, near_group) + part, F32),
@@ -372,7 +380,7 @@
     outs = pl.pallas_call(
         functools.partial(conv_kernel, group, width, poles),
         grid=(steps,),
-        in_specs=[big] * 4 + [par_spec] * 3 + [state_spec],
+        in_specs=[big] * 4 + [flat_spec] * 3 + [state_spec],
         out_specs=[big] * 4,
         out_shape=[jax.ShapeDtypeStruct((rows, features), BF16)] * 4,
         compiler_params=pltpu.CompilerParams(vmem_limit_bytes=limit),
@@ -381,10 +389,10 @@
         ),
         name="convolve",
     )(
-        query, key_in, value, cotangent, decay_rate, norm, residue,
+        query, key_in, value, cotangent, rates, norm, residues,
         entering.reshape(cores, 2, half, poles, width),
     )
-    return (*outs, res)
+    return (*outs, res.T)
 
 
 def solution(mesh):

time: 77.4 us -> 74.8 us (0.966)
  local copies, waits for them, and re-layouts: 3.53 us -> 0.61 us
    unnamed x5 -> x3, local copies, waits for them, and re-layouts: 3.53 us -> 0.61 us
where the time goes in v3:
time: 74.8 us; the launch traced here: 74.6 us
  Pallas kernels  72 us (96%)
  other arithmetic  1.32 us (2%)
    pallas_call x1, Pallas kernels, on_device(): pl.pallas_call(functools.partial(chain_kernel, near_group, rows), in_spec...  34.4 us
    pallas_call x1, Pallas kernels, on_device(): pl.pallas_call(functools.partial(conv_kernel, group, width, poles), grid=...  22.5 us
    pallas_call x1, Pallas kernels, on_device(): pl.pallas_call(functools.partial(state_kernel, group, width, poles, share...  15.2 us

profile of v3, /device:TPU:0, one launch (start us, length us, event | category | flops | bytes accessed | tf_op | source)
XLA Modules:
  0.0 74.6 jit_solution(5803267793901794437)
XLA Ops:
  0.6 1.3 %negate_sqrt_fusion.norm_ref = f32[16,48]{1,0:T(8,128)} fusion(f32[48,16]{0,1:T(8,128)} %param.10), kind=kLoop, calls=%fused_computation | loop fusion | flops 1536 | bytes 6144 | tf_op jit(solution)/shard_map/sqrt | solution.py:303
  1.9 15.2 %states.1 = (f32[2,2,24,16,128]{4,3,2,1,0:T(8,128)}, f32[48,16]{1,0:T(8,128)}, f32[2,24,16,128]{3,2,1,0:T(8,128)}) custom-call(bf16[192,6144]{1,0:T(8,128)(2,1)} %q_ref.3, bf16[192,6144]{1,0:T(8,128)(2,1)} %k_ref.3, bf16[192,6144]{1,0:T(8,128)(2,1)} %v_ref.3, bf16[192,6144]{1,0:T(8,128)(2,1)} %c_ref.3, f32[16,48]{1,0:T(8,128)} %bitcast.10, ...), custom_call_target="tpu_custom_call" | custom-call | flops 2264924160 | bytes 9437184 | tf_op jit(solution)/shard_map/states/pallas_call | solution.py:317
  17.2 34.4 %chain.1 = (f32[2,2,4,6,16,128]{5,4,3,2,1,0:T(8,128)}, f32[16,24]{1,0:T(8,128)}) custom-call(f32[2,2,4,6,16,128]{5,4,3,2,1,0:T(8,128)} %bitcast.8, f32[2,24,16]{2,1,0:T(8,128)} %bitcast.12, f32[2,4,6,16,128]{4,3,2,1,0:T(8,128)} %bitcast.9), custom_call_target="tpu_custom_call" | custom-call | tf_op jit(solution)/shard_map/chain/pallas_call | solution.py:344
  51.5 0.0 copy-start
  51.5 22.5 %convolve.1 = (bf16[192,6144]{1,0:T(8,128)(2,1)}, bf16[192,6144]{1,0:T(8,128)(2,1)}, bf16[192,6144]{1,0:T(8,128)(2,1)}, bf16[192,6144]{1,0:T(8,128)(2,1)}) custom-call(bf16[192,6144]{1,0:T(8,128)(2,1)} %q_ref.3, bf16[192,6144]{1,0:T(8,128)(2,1)} %k_ref.3, bf16[192,6144]{1,0:T(8,128)(2,1)} %v_ref.3, bf16[192,6144]{1,0:T(8,128)(2,1)} %c_ref.3, ...), custom_call_target="tpu_custom_call" | custom-call | flops 3623878656 | bytes 18874368 | tf_op jit(solution)/shard_map/convolve/pallas_call | solution.py:380
  74.0 0.0 copy-done
  74.0 0.6 copy.12
Async XLA Ops:
  51.5 22.5 %copy-start = (f32[16,24]{1,0:T(8,128)S(1)}, f32[16,24]{1,0:T(8,128)}, u32[]{:S(2)}) copy-start(f32[16,24]{1,0:T(8,128)} %get-tuple-element.22) | copy-start | bytes 4612
